TPU v7x, 32 devices: a whole 2x2x4 slice. The times are simulated.
32 devices in a mesh: dp: 8 (over z, y), seq: 4 (over x, core).
Axes of the slice: x: 2, y: 2, z: 4, core: 2. Of those that a mesh axis runs over, the one named last changes fastest.
Arguments:
- inputs: bfloat16 [32, 1024, 768], P('dp', 'seq'), may hold values from -6 to 6
- segments: int32 [32, 1024], P('dp', 'seq'), may hold values from 0 to 7, as said below
- teacher: bfloat16 [32, 1024, 768], P('dp', 'seq'), may hold values from -12 to 12
- mixing_weight: float32 [768, 2304], P('dp'), may hold values from -0.15625 to 0.15625
- output_weight: float32 [768, 768], P('dp'), may hold values from -1.75 to 1.75
- expand_weight: float32 [768, 3072], P('dp'), may hold values from -0.21875 to 0.21875
- shrink_weight: float32 [3072, 768], P('dp'), may hold values from -0.109375 to 0.109375
- vectors: float32 [9216], P('dp'), may hold values from -0.6 to 3.9
- mixing_first: float32 [768, 2304], P('dp'), may hold values from -0.3125 to 0.3125
- output_first: float32 [768, 768], P('dp'), may hold values from -0.3125 to 0.3125
- expand_first: float32 [768, 3072], P('dp'), may hold values from -0.3125 to 0.3125
- shrink_first: float32 [3072, 768], P('dp'), may hold values from -0.3125 to 0.3125
- vectors_first: float32 [9216], P('dp'), may hold values from -1.25 to 1.25
- mixing_second: float32 [768, 2304], P('dp'), may hold values from 0.00025 to 0.001
- output_second: float32 [768, 768], P('dp'), may hold values from 0.00025 to 0.001
- expand_second: float32 [768, 3072], P('dp'), may hold values from 0.00025 to 0.001
- shrink_second: float32 [3072, 768], P('dp'), may hold values from 0.00025 to 0.001
- vectors_second: float32 [9216], P('dp'), may hold values from 0.004 to 0.016
Outputs:
- block_output: bfloat16 [32, 1024, 768], P('dp', 'seq')
- input_grad: bfloat16 [32, 1024, 768], P('dp', 'seq')
- grad_norm: float32 [], replicated
- mixing_updated: float32 [768, 2304], P('dp')
- output_updated: float32 [768, 768], P('dp')
- expand_updated: float32 [768, 3072], P('dp')
- shrink_updated: float32 [3072, 768], P('dp')
- vectors_updated: float32 [9216], P('dp')
- mixing_momentum: float32 [768, 2304], P('dp')
- output_momentum: float32 [768, 768], P('dp')
- expand_momentum: float32 [768, 3072], P('dp')
- shrink_momentum: float32 [3072, 768], P('dp')
- vectors_momentum: float32 [9216], P('dp')
- mixing_variance: float32 [768, 2304], P('dp')
- output_variance: float32 [768, 768], P('dp')
- expand_variance: float32 [768, 3072], P('dp')
- shrink_variance: float32 [3072, 768], P('dp')
- vectors_variance: float32 [9216], P('dp')
Inputs may be any that keep to these rules, and one draw needn't show every extreme that they name: `segments`: along each packed row the ids never fall and number its documents from 0 in order; of the packed rows of each index of dp, one holds a single document and the others hold 8 documents each.
All inputs are finite; a program needn't handle non-finite values.
Results may differ from a plain program's by a relative error of at most 0.018.
The roundings to bfloat16 on the way count: a program that leaves them out, or rounds other values in their place, can miss the bound.
Values may be sent and summed in bfloat16 or wider, within the bound.
A program may use at most 256 MiB of HBM per device.

v0:
```python
from functools import partial
import math

import jax
import jax.numpy as jnp
from jax import lax
from jax.experimental import pallas as pl
from jax.experimental.pallas import tpu as pltpu
from jax.sharding import PartitionSpec as P

D = 768
HEADS = 12
HD = 64
FF = 3072
LEN = 1024
NDOC = 8
STEP = 10


NEGATIVE = -1e30
NORM_EPS = 1e-05
BETA_ONE = 0.9
BETA_TWO = 0.999
ADAM_EPS = 1e-08
WEIGHT_DECAY = 0.01


def layer_norm(values, norm_gain, norm_shift):
    center = values - jnp.mean(values, axis=-1, keepdims=True)
    spread = jnp.mean(center * center, axis=-1, keepdims=True)
    return center * lax.rsqrt(spread + NORM_EPS) * norm_gain + norm_shift


def gelu_tanh(values):
    return jax.nn.gelu(values, approximate=True)


def split_vectors(packed):
    return jnp.split(packed, [D, 2 * D, 3 * D, 4 * D, 5 * D, 6 * D, 7 * D, 7 * D + FF])


def adamw(master, first, second, gradient, rate):
    first_new = BETA_ONE * first + (1.0 - BETA_ONE) * gradient
    second_new = BETA_TWO * second + (1.0 - BETA_TWO) * gradient * gradient
    first_hat = first_new / (1.0 - BETA_ONE**STEP)
    second_hat = second_new / (1.0 - BETA_TWO**STEP)
    updated = master - rate * (
        first_hat / (jnp.sqrt(second_hat) + ADAM_EPS) + WEIGHT_DECAY * master
    )
    return (updated, first_new, second_new)


def learn_rates():
    return (
        1.0 / math.sqrt(2 * D),
        1.0 / math.sqrt(max(1, 2 * D * NDOC // LEN)),
        1.0 / math.sqrt(D),
        1.0 / math.sqrt(FF),
        0.3,
    )


def clip_level():
    return 0.5 * math.sqrt(4 * D * D + 2 * D * FF + 8 * D + FF)


def visible(query_pos, key_pos, query_seg, key_seg):
    return (key_pos[None, :] <= query_pos[:, None]) & (key_seg[None, :] == query_seg[:, None])


def attend_rows(query_pos, key_pos, packed_args):
    queries, keys_all, values_all, query_seg, key_seg = packed_args
    scores = jnp.einsum("qhd,khd->hqk", queries, keys_all, preferred_element_type=jnp.float32)
    scores = jnp.where(visible(query_pos, key_pos, query_seg, key_seg)[None], scores, NEGATIVE)
    top_score = jnp.max(scores, axis=-1, keepdims=True)
    exponent = jnp.exp(scores - top_score)
    totals = jnp.sum(exponent, axis=-1, keepdims=True)
    probability = (exponent / totals).astype(jnp.bfloat16)
    attended = jnp.einsum(
        "hqk,khd->qhd", probability, values_all, preferred_element_type=jnp.float32
    )
    return (attended, (top_score + jnp.log(totals))[..., 0])


def attend_back(query_pos, key_pos, packed_args):
    queries, keys_all, values_all, upstream, log_totals, query_seg, key_seg = packed_args
    scores = jnp.einsum("qhd,khd->hqk", queries, keys_all, preferred_element_type=jnp.float32)
    scores = jnp.where(visible(query_pos, key_pos, query_seg, key_seg)[None], scores, NEGATIVE)
    probability = jnp.exp(scores - log_totals[..., None])
    prob_low = probability.astype(jnp.bfloat16)
    prob_grad = jnp.einsum("qhd,khd->hqk", upstream, values_all, preferred_element_type=jnp.float32)
    value_part = jnp.einsum("hqk,qhd->khd", prob_low, upstream, preferred_element_type=jnp.float32)
    score_grad = probability * (
        prob_grad - jnp.sum(probability * prob_grad, axis=-1, keepdims=True)
    )
    score_low = score_grad.astype(jnp.bfloat16)
    query_part = jnp.einsum("hqk,khd->qhd", score_low, keys_all, preferred_element_type=jnp.float32)
    key_part = jnp.einsum("hqk,qhd->khd", score_low, queries, preferred_element_type=jnp.float32)
    key_count = keys_all.shape[0]
    return (
        query_part,
        jnp.concatenate(
            [key_part.reshape(key_count, -1), value_part.reshape(key_count, -1)], axis=1
        ),
    )


def body(
    inputs,
    segments,
    teacher,
    mixing_weight,
    output_weight,
    expand_weight,
    shrink_weight,
    vectors,
    mixing_first,
    output_first,
    expand_first,
    shrink_first,
    vectors_first,
    mixing_second,
    output_second,
    expand_second,
    shrink_second,
    vectors_second,
):
    bfloat = jnp.bfloat16
    floats = jnp.float32
    seq_count, local_len, features = inputs.shape
    row_count = seq_count * local_len
    scale = 1.0 / math.sqrt(HD)
    mixing_low, output_low, expand_low, shrink_low, vectors_low = (
        lax.all_gather(mixing_weight.astype(bfloat), "dp", axis=0, tiled=True),
        lax.all_gather(output_weight.astype(bfloat), "dp", axis=0, tiled=True),
        lax.all_gather(expand_weight.astype(bfloat), "dp", axis=0, tiled=True),
        lax.all_gather(shrink_weight.astype(bfloat), "dp", axis=0, tiled=True),
        lax.all_gather(vectors.astype(bfloat), "dp", axis=0, tiled=True),
    )
    (
        gain_one,
        shift_one,
        bias_query,
        bias_value,
        bias_output,
        gain_two,
        shift_two,
        bias_expand,
        bias_shrink,
    ) = split_vectors(vectors_low.astype(floats))
    states = inputs.astype(floats).reshape(row_count, features)
    normed = layer_norm(states, gain_one, shift_one)
    normed_low = normed.astype(bfloat)
    projected = jnp.dot(normed_low, mixing_low, preferred_element_type=floats)
    query_low = ((projected[:, :features] + bias_query) * scale).astype(bfloat)
    key_low = projected[:, features : 2 * features].astype(bfloat)
    value_low = (projected[:, 2 * features :] + bias_value).astype(bfloat)
    key_all, value_all = (
        lax.all_gather(key_low.reshape(seq_count, local_len, features), "seq", axis=1, tiled=True),
        lax.all_gather(
            value_low.reshape(seq_count, local_len, features), "seq", axis=1, tiled=True
        ),
    )
    segment_all = lax.all_gather(segments, "seq", axis=1, tiled=True)
    full_len = key_all.shape[1]
    query_pos = lax.axis_index("seq") * local_len + jnp.arange(local_len, dtype=jnp.int32)
    key_pos = jnp.arange(full_len, dtype=jnp.int32)
    query_heads = query_low.reshape(seq_count, local_len, HEADS, HD)
    key_heads = key_all.reshape(seq_count, full_len, HEADS, HD)
    value_heads = value_all.reshape(seq_count, full_len, HEADS, HD)
    attended, log_totals = lax.map(
        partial(attend_rows, query_pos, key_pos),
        (query_heads, key_heads, value_heads, segments, segment_all),
    )
    attended_low = attended.reshape(row_count, features).astype(bfloat)
    middle = states + jnp.dot(attended_low, output_low, preferred_element_type=floats) + bias_output
    normed_two = layer_norm(middle, gain_two, shift_two)
    normed_two_low = normed_two.astype(bfloat)
    hidden = jnp.dot(normed_two_low, expand_low, preferred_element_type=floats) + bias_expand
    active, gelu_back = jax.vjp(gelu_tanh, hidden)
    active_low = active.astype(bfloat)
    result = middle + jnp.dot(active_low, shrink_low, preferred_element_type=floats) + bias_shrink
    block_output = result.astype(bfloat).reshape(seq_count, local_len, features)
    target_prob = jax.nn.softmax(teacher.astype(floats).reshape(row_count, features), axis=-1)
    result_grad = features * (jax.nn.softmax(result, axis=-1) - target_prob)
    result_low = result_grad.astype(bfloat)
    grad_shrink = jnp.dot(active_low.T, result_low, preferred_element_type=floats)
    grad_bias_shrink = jnp.sum(result_grad, axis=0)
    active_grad = jnp.dot(result_low, shrink_low.T, preferred_element_type=floats)
    active_round = lax.optimization_barrier(active_grad.astype(bfloat)).astype(floats)
    hidden_low = gelu_back(active_round)[0].astype(bfloat)
    grad_bias_expand = jnp.sum(hidden_low.astype(floats), axis=0)
    grad_expand = jnp.dot(normed_two_low.T, hidden_low, preferred_element_type=floats)
    normed_two_grad = jnp.dot(hidden_low, expand_low.T, preferred_element_type=floats)
    norm_two_back = jax.vjp(layer_norm, middle, gain_two, shift_two)[1]
    middle_part, grad_gain_two, grad_shift_two = norm_two_back(normed_two_grad)
    middle_grad = result_grad + middle_part
    middle_low = middle_grad.astype(bfloat)
    grad_bias_output = jnp.sum(middle_grad, axis=0)
    grad_output = jnp.dot(attended_low.T, middle_low, preferred_element_type=floats)
    attended_grad = jnp.dot(middle_low, output_low.T, preferred_element_type=floats).astype(bfloat)
    upstream_heads = attended_grad.reshape(seq_count, local_len, HEADS, HD)
    query_grad, kv_terms = lax.map(
        partial(attend_back, query_pos, key_pos),
        (query_heads, key_heads, value_heads, upstream_heads, log_totals, segments, segment_all),
    )
    kv_sums = (
        lax.psum_scatter(kv_terms.astype(jnp.bfloat16), "seq", scatter_dimension=1, tiled=True)
        .astype(jnp.float32)
        .reshape(row_count, 2 * features)
    )
    key_grad_low = kv_sums[:, :features].astype(bfloat)
    value_grad_low = kv_sums[:, features:].astype(bfloat)
    query_grad_low = query_grad.reshape(row_count, features).astype(bfloat)
    query_scaled = query_grad_low.astype(floats) * scale
    grad_bias_query = jnp.sum(query_scaled, axis=0)
    grad_bias_value = jnp.sum(value_grad_low.astype(floats), axis=0)
    projected_grad = jnp.concatenate(
        [query_scaled.astype(bfloat), key_grad_low, value_grad_low], axis=1
    )
    grad_mixing = jnp.dot(normed_low.T, projected_grad, preferred_element_type=floats)
    normed_grad = jnp.dot(projected_grad, mixing_low.T, preferred_element_type=floats)
    norm_one_back = jax.vjp(layer_norm, states, gain_one, shift_one)[1]
    states_part, grad_gain_one, grad_shift_one = norm_one_back(normed_grad)
    input_grad = (middle_grad + states_part).astype(bfloat).reshape(seq_count, local_len, features)
    grad_vectors = jnp.concatenate(
        [
            grad_gain_one,
            grad_shift_one,
            grad_bias_query,
            grad_bias_value,
            grad_bias_output,
            grad_gain_two,
            grad_shift_two,
            grad_bias_expand,
            grad_bias_shrink,
        ]
    )
    vector_rows = grad_vectors.reshape(lax.axis_size("dp"), -1)
    mixing_part, output_part, expand_part, shrink_part, vector_part = (
        lax.psum_scatter(
            grad_mixing.astype(jnp.bfloat16), "dp", scatter_dimension=0, tiled=True
        ).astype(jnp.float32),
        lax.psum_scatter(
            grad_output.astype(jnp.bfloat16), "dp", scatter_dimension=0, tiled=True
        ).astype(jnp.float32),
        lax.psum_scatter(
            grad_expand.astype(jnp.bfloat16), "dp", scatter_dimension=0, tiled=True
        ).astype(jnp.float32),
        lax.psum_scatter(
            grad_shrink.astype(jnp.bfloat16), "dp", scatter_dimension=0, tiled=True
        ).astype(jnp.float32),
        lax.psum_scatter(
            vector_rows.astype(jnp.bfloat16), "dp", scatter_dimension=0, tiled=True
        ).astype(jnp.float32),
    )
    mixing_sum, output_sum, expand_sum, shrink_sum, vector_sum = (
        lax.psum(mixing_part.astype(jnp.bfloat16), "seq").astype(jnp.float32),
        lax.psum(output_part.astype(jnp.bfloat16), "seq").astype(jnp.float32),
        lax.psum(expand_part.astype(jnp.bfloat16), "seq").astype(jnp.float32),
        lax.psum(shrink_part.astype(jnp.bfloat16), "seq").astype(jnp.float32),
        lax.psum(vector_part.astype(jnp.bfloat16), "seq").astype(jnp.float32),
    )
    vector_sum = vector_sum.reshape(-1)
    squares = (
        jnp.sum(mixing_sum * mixing_sum)
        + jnp.sum(output_sum * output_sum)
        + jnp.sum(expand_sum * expand_sum)
        + jnp.sum(shrink_sum * shrink_sum)
        + jnp.sum(vector_sum * vector_sum)
    )
    grad_norm = jnp.sqrt(lax.psum(squares, "dp"))
    clip_value = clip_level()
    factor = clip_value / jnp.maximum(grad_norm, clip_value)
    step_rates = learn_rates()
    mixing_new = adamw(
        mixing_weight, mixing_first, mixing_second, mixing_sum * factor, step_rates[0]
    )
    output_new = adamw(
        output_weight, output_first, output_second, output_sum * factor, step_rates[1]
    )
    expand_new = adamw(
        expand_weight, expand_first, expand_second, expand_sum * factor, step_rates[2]
    )
    shrink_new = adamw(
        shrink_weight, shrink_first, shrink_second, shrink_sum * factor, step_rates[3]
    )
    vectors_new = adamw(vectors, vectors_first, vectors_second, vector_sum * factor, step_rates[4])
    return (
        block_output,
        input_grad,
        grad_norm,
        mixing_new[0],
        output_new[0],
        expand_new[0],
        shrink_new[0],
        vectors_new[0],
        mixing_new[1],
        output_new[1],
        expand_new[1],
        shrink_new[1],
        vectors_new[1],
        mixing_new[2],
        output_new[2],
        expand_new[2],
        shrink_new[2],
        vectors_new[2],
    )

MESH = pl.DeviceIdType.MESH
BF = jnp.bfloat16
F32 = jnp.float32
BLK = 256
NN = ((1,), (0,))
NT = ((1,), (1,))
TN = ((0,), (0,))
VMEM_BYTES = 64 * 2**20 - 2**17
VROWS = 16
MIX, OUT, EXP, SHR = 0, 1, 2, 3
HALF = D // 2
PAIRS = D // 128
EXPAND_TILE = D
SUBS = (4, 1, 2, 2)
LANES = (0, 4, 5, 7)


def dot(left, right, dims):
    return lax.dot_general(left, right, (dims, ((), ())), preferred_element_type=F32)


class Place:
    def __init__(self, count):
        self.count = count
        self.hops = (count // 2, count - 1 - count // 2)
        self.dp = lax.axis_index("dp")
        self.seq = lax.axis_index("seq")
        odd = self.dp % 2
        self.pos = (1 - odd) * (self.dp // 2) + odd * (count - 1 - self.dp // 2)
        self.core = self.seq % 2
        self.x = self.seq // 2
        self.step = 1 - 2 * self.core
        self.sides = ((self.ahead(1), self.seq), (self.behind(1), self.seq))
        self.mate = self.kin(1)
        self.across = self.kin(2)

    def at(self, pos):
        pos = pos % self.count
        upper = pos // (self.count // 2)
        return (1 - upper) * (2 * pos) + upper * (2 * (self.count - 1 - pos) + 1)

    def ahead(self, steps):
        return self.at(self.pos + steps * self.step + self.count)

    def behind(self, steps):
        return self.at(self.pos - steps * self.step + self.count)

    def kin(self, which):
        core = self.core + (1 - 2 * self.core) * (which % 2)
        return (self.dp, 2 * (self.x + (1 - 2 * self.x) * (which // 2)) + core)

    def dp_peer(self, offset):
        return ((self.dp + offset) % self.count, self.seq)

    def greet(self):
        barrier = pltpu.get_barrier_semaphore()
        peers = [self.kin(k) for k in range(1, 4)]
        peers += [self.dp_peer(k) for k in range(1, self.count)]
        for peer in peers:
            pl.semaphore_signal(barrier, inc=1, device_id=peer, device_id_type=MESH)
        return lambda: pl.semaphore_wait(barrier, len(peers))


def describe(src, dst, send, recv, device):
    return pltpu.make_async_remote_copy(
        src_ref=src,
        dst_ref=dst,
        send_sem=send,
        recv_sem=recv,
        device_id=device,
        device_id_type=MESH,
    )


def remote(src, dst, send, recv, device):
    copy = describe(src, dst, send, recv, device)
    copy.start()
    return copy


def local(src, dst, sem):
    copy = pltpu.make_async_copy(src, dst, sem)
    copy.start()
    return copy


def span(start, size, unit):
    return pl.ds(start if isinstance(start, int) else pl.multiple_of(start, unit), size)


def spread(ticks, marks):
    def at(trip, mark, first=0, past=None):
        for n in range(first, len(ticks) // marks if past is None else past):
            here = ticks[n * marks + mark]
            if here:

                def run(here=here):
                    for tick in here:
                        tick()

                pl.when(trip == n)(run)

    return at


class Group:
    def __init__(self, send, recv, of_all_sent, of_all_received, device):
        self.send, self.recv, self.device = send, recv, device
        self.bytes = (of_all_sent, of_all_received)

    def start(self, src, dst, device):
        describe(src, dst, self.send, self.recv, device).start()

    def all(self, which):
        return describe(self.bytes[which], self.bytes[which], self.send, self.recv, self.device)

    def wait_recv(self):
        self.all(1).wait_recv()

    def wait_send(self):
        self.all(0).wait_send()


class Gather:
    def __init__(self, place, full, sems):
        self.place, self.full = place, full
        self.ring_s, self.ring_r, self.mate_s, self.mate_r, self.cross_s, self.cross_r = sems

    def lanes(self, w):
        return ((0, 1), (0,), (self.place.x, 2), (self.place.x, 2, 3))[w]

    def part(self, ref, w, sub):
        rows, columns = ref.shape[-2:]
        lead = (slice(None),) * (len(ref.shape) - 2)
        if w == SHR:
            unit = rows // 6
            if isinstance(sub, int) and sub >= 2:
                return ref.at[lead + (pl.ds((2 * sub - 2) * unit, 2 * unit),)]
            return ref.at[lead + (span(sub * unit, unit, 16),)]
        unit = columns // (2, 1, 3)[w]
        return ref.at[lead + (slice(None), span(sub * unit, unit, 128))]

    def cut(self, w, owner, core, sub):
        return self.part(self.full[w].at[owner, core], w, sub)

    def block(self, w, sub, way, t):
        owner = self.place.ahead(t) if way else self.place.behind(t)
        return self.cut(w, owner, self.place.core, sub)

    def copy(self, block, send, recv, device):
        return describe(block, block, send, recv, device)

    def ring(self, w, lane, way, t):
        index = ((0, 2, 3, 5)[w] + lane, t + way * self.place.hops[0])
        block = self.block(w, self.lanes(w)[lane], way, t)
        return self.copy(block, self.ring_s.at[w], self.ring_r.at[index], self.place.sides[way])

    def pair(self, w, sub, way, t):
        block = self.block(w, sub, way, t)
        return self.copy(block, self.mate_s.at[w], self.mate_r.at[w], self.place.mate)

    def over(self, w, way, t):
        recv = self.cross_r.at[w - EXP, t - 1 + way * self.place.hops[0]]
        block = self.block(w, self.place.x, way, t)
        return self.copy(block, self.cross_s.at[w - EXP], recv, self.place.across)

    def start(self, w):
        for lane in range(len(self.lanes(w))):
            for way in range(2):
                self.ring(w, lane, way, 0).start()

    def tick(self, w, lane, way, t):
        self.ring(w, lane, way, t - 1).wait_recv()
        if t < self.place.hops[way]:
            self.ring(w, lane, way, t).start()
        self.pair(w, self.lanes(w)[lane], way, t).start()
        if w >= EXP and lane == 0:
            self.over(w, way, t).start()

    def relay(self, w, way, t):
        self.over(w, way, t).wait_recv()
        self.pair(w, 1 - self.place.x, way, t).start()

    def others(self, w):
        return self.full[w].at[pl.ds(0, self.place.count - 1), self.place.core]

    def arrived(self, w):
        block = self.others(w)
        self.copy(block, self.mate_s.at[w], self.mate_r.at[w], self.place.mate).wait_recv()

    def drain(self, w):
        block = self.others(w)
        self.copy(block, self.mate_s.at[w], self.mate_r.at[w], self.place.mate).wait_send()
        if w >= EXP:
            for lane in range(len(self.lanes(w))):
                part = self.part(block, w, self.lanes(w)[lane])
                self.copy(part, self.ring_s.at[w], self.mate_r.at[w], self.place.mate).wait_send()
            part = self.part(block, w, 0)
            self.copy(part, self.cross_s.at[w - EXP], self.mate_r.at[w], self.place.across).wait_send()
        else:
            self.copy(block, self.ring_s.at[w], self.mate_r.at[w], self.place.mate).wait_send()


class Scatter:
    def __init__(self, place, grads, mates, slots, sums, sems):
        self.place, self.grads, self.mates, self.slots = place, grads, mates, slots
        self.sums = sums
        (
            self.mate_s,
            self.mate_r,
            self.ring_s,
            self.ring_r,
            self.cross_s,
            self.cross_r,
            self.total_s,
            self.total_r,
        ) = sems

    def cut(self, ref, w, sub):
        rows, columns = ref.shape[-2:]
        lead = (slice(None),) * (len(ref.shape) - 2)
        if w == SHR:
            return ref.at[lead + (span(sub * (rows // 2), rows // 2, 16),)]
        if w == MIX:
            rows = self.sums[w].shape[1]
            there = pl.ds((sub - 1) * (rows // 3), rows // 3) if sub else pl.ds(0, rows)
            return ref.at[lead + (there, pl.ds(HALF if sub else 0, HALF))]
        size = columns // SUBS[w]
        return ref.at[lead + (slice(None), span(sub * size, size, 128))]

    def owner(self, way, distance):
        return self.place.behind(distance) if way else self.place.ahead(distance)

    def own(self, w, owner, core, sub):
        return self.cut(self.grads[w].at[owner, core], w, sub)

    def slot(self, w, way, t, sub):
        return self.cut(self.slots(w, t + way * self.place.hops[0]), w, sub)

    def pair(self, w, sub, owner):
        return describe(
            self.own(w, owner, 1 - self.place.core, sub),
            self.cut(self.mates(w, owner), w, sub),
            self.mate_s.at[LANES[w] + sub],
            self.mate_r.at[LANES[w] + sub],
            self.place.mate,
        )

    def pairs(self, w, sub):
        block = self.cut(self.grads[w].at[:, self.place.core], w, sub)
        return describe(
            block, block, self.mate_s.at[LANES[w] + sub], self.mate_r.at[LANES[w] + sub], self.place.mate
        )

    def ring(self, w, sub, way, t):
        if t == 0:
            owner = self.owner(way, self.place.hops[way])
            src = self.own(w, owner, self.place.core, sub)
        else:
            src = self.slot(w, way, t - 1, sub)
        index = (LANES[w] + sub, t + way * self.place.hops[0])
        return describe(
            src,
            self.slot(w, way, t, sub),
            self.ring_s.at[LANES[w] + sub],
            self.ring_r.at[index],
            self.place.sides[way],
        )

    def over(self, w, sub):
        return describe(
            self.own(w, self.place.dp, self.place.core, sub),
            self.cut(self.sums[w].at[self.place.core], w, sub),
            self.cross_s.at[LANES[w] + sub],
            self.cross_r.at[LANES[w] + sub],
            self.place.across,
        )

    def total(self, w, sub):
        block = self.cut(self.sums[w].at[self.place.core], w, sub)
        return describe(
            block, block, self.total_s.at[LANES[w] + sub], self.total_r.at[LANES[w] + sub], self.place.mate
        )

    def hand(self, w, sub):
        for owner in range(self.place.count):
            self.pair(w, sub, owner).start()

    def term(self, w, sub, way, distance):
        owner = self.owner(way, distance)
        mine = self.own(w, owner, self.place.core, sub)[...].astype(F32)
        return mine + self.cut(self.mates(w, owner), w, sub)[...].astype(F32)

    def start(self, w, sub):
        self.pairs(w, sub).wait_recv()
        for way, hops in enumerate(self.place.hops):
            term = self.term(w, sub, way, hops)
            self.own(w, self.owner(way, hops), self.place.core, sub)[...] = term.astype(BF)
            self.ring(w, sub, way, 0).start()

    def tick(self, w, sub, way, t):
        self.ring(w, sub, way, t - 1).wait_recv()
        slot = self.slot(w, way, t - 1, sub)
        term = self.term(w, sub, way, self.place.hops[way] - t)
        slot[...] = (slot[...].astype(F32) + term).astype(BF)
        self.ring(w, sub, way, t).start()

    def finish(self, w, sub):
        total = self.term(w, sub, 0, 0)
        for way, hops in enumerate(self.place.hops):
            self.ring(w, sub, way, hops - 1).wait_recv()
            total = total + self.slot(w, way, hops - 1, sub)[...].astype(F32)
        self.own(w, self.place.dp, self.place.core, sub)[...] = total.astype(BF)
        self.over(w, sub).start()

    def crossed(self, w, sub):
        self.over(w, sub).wait_recv()
        value = self.own(w, self.place.dp, self.place.core, sub)[...].astype(F32)
        there = self.cut(self.sums[w].at[self.place.core], w, sub)
        there[...] = (value + there[...].astype(F32)).astype(BF)
        self.total(w, sub).start()

    def arrived(self, w, sub):
        self.total(w, sub).wait_recv()

    def drain(self, w):
        for sub in range(SUBS[w]):
            self.pairs(w, sub).wait_send()
            sent = self.cut(self.grads[w].at[pl.ds(0, self.place.count - 1), self.place.core], w, sub)
            describe(
                sent, sent, self.ring_s.at[LANES[w] + sub], self.mate_r.at[LANES[w] + sub], self.place.mate
            ).wait_send()
            self.over(w, sub).wait_send()
            self.total(w, sub).wait_send()

    def ticks(self, w, t, subs):
        return [
            partial(self.tick, w, sub, way, t)
            for sub in subs
            for way, hops in enumerate(self.place.hops)
            if t < hops
        ]


def half_lanes(hd):
    lane = lax.broadcasted_iota(jnp.int32, (1, 128), 1)
    return (lane < 64) if hd == 0 else (lane >= 64)


def document_lanes(documents):
    lane = lax.broadcasted_iota(jnp.int32, documents.shape, 1) % 64
    same = jnp.logical_and(documents == lane.astype(F32), lane < 8)
    return jnp.where(same, 1.0, 0.0).astype(BF)


def marked_keys(keys, marked):
    hidden = ((1.0 - marked.astype(F32)) * NEGATIVE).astype(BF)
    return [jnp.where(half_lanes(hd), keys, hidden) for hd in range(2)]


def columns_of(hp):
    first = (hp // 3) * (3 * HALF) + (hp % 3) * 128
    return [span(first + part * HALF, 128, 128) for part in range(3)]


def attend_pair(hp, qkv, marked, causal, out, lse, scores, tick):
    cq, ck, cv = columns_of(hp)
    vt = qkv[:, cv].T
    ones = jnp.ones((8, vt.shape[1]), BF)
    keys = marked_keys(qkv[:, ck], marked[...])
    values = [jnp.concatenate([vt[hd * 64 : (hd + 1) * 64, :], ones], axis=0) for hd in range(2)]
    def rows_of(n):
        return slice(n * BLK, (n + 1) * BLK)

    def score(i, hd):
        kept = rows_of(hd)
        query = jnp.where(half_lanes(hd), qkv[rows_of(i), cq], marked[rows_of(i), :])
        top = None
        for j in range(i + 1):
            s = dot(keys[hd][rows_of(j), :], query, NT)
            if i == j:
                s = s + causal[...]
            scores[rows_of(j), kept] = s
            best = jnp.max(s, axis=0, keepdims=True)
            top = best if top is None else jnp.maximum(top, best)
        return top

    def weigh(i, hd, top):
        parts = [
            jnp.exp(scores[rows_of(j), rows_of(hd)] - top).astype(BF) for j in range(i + 1)
        ]
        return i, hd, top, parts

    outs = []

    def collect(i, hd, top, parts):
        acc = None
        for j, p in enumerate(parts):
            term = dot(values[hd][:, rows_of(j)], p, NN)
            acc = term if acc is None else acc + term
        total = acc[64:65, :]
        lse[pl.ds(hp * 2 + hd, 1), rows_of(i)] = top + jnp.log(total)
        outs.append(acc[0:64, :] * (1.0 / total))
        if hd == 1:
            out[rows_of(i), span(hp * 128, 128, 128)] = (
                jnp.concatenate(outs, axis=0).T.astype(BF)
            )
            outs[:] = []

    chains = [(i, hd) for i in range(qkv.shape[0] // BLK) for hd in range(2)]
    tick(0)
    top = score(*chains[0])
    behind = None
    for n, (i, hd) in enumerate(chains):
        after = None
        if n + 1 < len(chains):
            if hd == 1:
                tick(i + 1)
            after = score(*chains[n + 1])
        if behind is not None:
            collect(*behind)
        behind = weigh(i, hd, top)
        top = after
    collect(*behind)


def attend_back_pair(hp, qkv, marked, causal, out, upstream, lse, sums, tick):
    cq, ck, cv = columns_of(hp)
    co = span(hp * 128, 128, 128)
    in_v, in_k = slice(0, 128), slice(128, 256)
    kt = qkv[:, ck].T
    keys = marked_keys(qkv[:, ck], marked[...])
    def rows_of(n):
        return slice(n * BLK, (n + 1) * BLK)

    def operands(i):
        qb = qkv[rows_of(i), cq]
        db = upstream[rows_of(i), co]
        none = jnp.zeros_like(qb)
        prod = (db.astype(F32) * out[rows_of(i), co].astype(F32)).T
        queries = [jnp.where(half_lanes(hd), qb, marked[rows_of(i), :]) for hd in range(2)]
        grads = [jnp.where(half_lanes(hd), db, none) for hd in range(2)]
        return (
            queries,
            grads,
            [jnp.sum(prod[hd * 64 : (hd + 1) * 64, :], axis=0, keepdims=True) for hd in range(2)],
            [lse[pl.ds(hp * 2 + hd, 1), rows_of(i)] for hd in range(2)],
            jnp.concatenate([jnp.where(half_lanes(hd), qb, none) for hd in range(2)], axis=0),
            jnp.concatenate(grads, axis=0),
        )

    def products(n, ops):
        i, j = blocks[n]
        kept = slice((1 + n % 2) * BLK, (2 + n % 2) * BLK)
        for hd in range(2):
            s = dot(keys[hd][rows_of(j), :], ops[0][hd], NT)
            sums[rows_of(hd), kept] = s + causal[...] if i == j else s
            sums[rows_of(2 + hd), kept] = dot(qkv[rows_of(j), cv], ops[1][hd], NT)

    blocks = [(i, j) for i in range(qkv.shape[0] // BLK) for j in range(i + 1)]
    tick(0)
    ops = operands(0)
    products(0, ops)
    dqs = [None, None]

    def gather_block(i, j, now, ps, dss):
        for hd in range(2):
            term = dot(kt[hd * 64 : (hd + 1) * 64, rows_of(j)], dss[hd], NN)
            dqs[hd] = term if dqs[hd] is None else dqs[hd] + term
        pv = dot(jnp.concatenate(ps, axis=1), now[5], NN)
        pk = dot(jnp.concatenate(dss, axis=1), now[4], NN)
        if i == j:
            sums[rows_of(j), in_v] = pv
            sums[rows_of(j), in_k] = pk
            low = jnp.concatenate(dqs, axis=0).T.astype(BF).astype(F32)
            qkv[rows_of(i), cq] = (low * (1.0 / math.sqrt(HD))).astype(BF)
            dqs[:] = [None, None]
        else:
            sums[rows_of(j), in_v] += pv
            sums[rows_of(j), in_k] += pk

    behind = None
    for n, (i, j) in enumerate(blocks):
        now = ops
        kept = slice((1 + n % 2) * BLK, (2 + n % 2) * BLK)
        if n + 1 < len(blocks):
            if blocks[n + 1][1] == 0:
                tick(i + 1)
                ops = operands(i + 1)
            products(n + 1, ops)
        if behind is not None:
            gather_block(*behind)
        ps, dss = [], []
        for hd in range(2):
            p = jnp.exp(sums[rows_of(hd), kept] - now[3][hd])
            ps.append(p.astype(BF))
            dss.append((p * (sums[rows_of(2 + hd), kept] - now[2][hd])).astype(BF))
        behind = (i, j, now, ps, dss)
    gather_block(*behind)
    qkv[:, ck] = sums[:, in_k].astype(BF)
    qkv[:, cv] = sums[:, in_v].astype(BF)


def normalised(values):
    center = values - jnp.mean(values, axis=-1, keepdims=True)
    inverse = lax.rsqrt(jnp.mean(center * center, axis=-1, keepdims=True) + NORM_EPS)
    return center * inverse, inverse


def norm_grad(values, gain, upstream):
    hat, inverse = normalised(values)
    scaled = upstream * gain
    first = jnp.mean(scaled, axis=-1, keepdims=True)
    second = jnp.mean(scaled * hat, axis=-1, keepdims=True)
    return (
        inverse * (scaled - first - hat * second),
        jnp.sum(upstream * hat, axis=0, keepdims=True),
        jnp.sum(upstream, axis=0, keepdims=True),
    )


def gelu_both(u):
    inner = math.sqrt(2.0 / math.pi)
    cubic = inner * 0.044715
    square = u * u
    half = 0.5 + 0.5 * jnp.tanh(u * (inner + cubic * square))
    value = u * half
    return value, half + value * (1.0 - half) * (2.0 * inner + 6.0 * cubic * square)


def softmax(values):
    e = jnp.exp(values - jnp.max(values, axis=-1, keepdims=True))
    return e * (1.0 / jnp.sum(e, axis=-1, keepdims=True))


def whole(ref):
    return ref[...].reshape(-1, ref.shape[-1])


VEC_PLACES = (("g1", D), ("b1", D), ("bq", D), ("bv", D), ("bo", D), ("g2", D), ("b2", D), ("bf1", FF), ("bf2", D))
VEC_ROW = {name: row for row, (name, _) in enumerate(VEC_PLACES)}
VEC_SIZE = dict(VEC_PLACES)


def block_kernel(count, *refs):
    inputs, teacher, segments, masters, vec_ref = refs[0], refs[1], refs[2], refs[3:7], refs[7]
    sums, vec_sum, norm_ref, out_rows, back_rows = refs[8:12], refs[12], refs[13], refs[14], refs[15]
    (
        full0, full1, full2, full3, x, h1, qkv, att, x1, h2, act, slope, dy, low, sent, shrink_grads,
        shr_mate, shr_slot, lse, segs, seg_stage, marked, causal,
        vec_stage, vec_all, vec, gvec, vec_out, vec_buf, vec_mine, vec_seq, sq_mine, sq_buf,
        load_sem, g_ring_s, g_ring_r, g_mate_s, g_mate_r, g_cross_s, g_cross_r,
        s_mate_s, s_mate_r, s_ring_s, s_ring_r, s_cross_s, s_cross_r, s_total_s, s_total_r,
        row_s, row_r, row_l, vec_s, vec_r, free,
    ) = refs[16:]
    full = (full0, full1, full2, full3)
    place = Place(count)
    ready = place.greet()
    length = x.shape[0]
    blocks = length // BLK
    scale = 1.0 / math.sqrt(HD)

    def rows(i):
        return span(i * BLK, BLK, BLK)

    loads, pieces, used = [], [], [0, 0]
    for w in (MIX, OUT, EXP, SHR):
        height, width = masters[w].shape
        for column in range(0, width, D):
            which = 0 if used[0] + height <= length else 1
            where = (dy, x1)[which].at[pl.ds(used[which], height)]
            used[which] += height
            source = masters[w].at[:, pl.ds(column, D)]
            loads.append(local(source, where, load_sem.at[len(loads)]))
            pieces.append((w, column, where))

    def stage(w):
        for load, (owner, column, where) in zip(loads, pieces):
            if owner == w:
                load.wait()
                piece = where[...].astype(BF).reshape(full[w].shape[1:3] + (D,))
                if w == MIX:
                    for part in range(2):
                        c = slice(part * HALF, (part + 1) * HALF)
                        there = pl.ds(part * 3 * HALF + column // 2, HALF)
                        full[w][place.dp, :, :, there] = piece[:, :, c]
                else:
                    full[w][place.dp, :, :, pl.ds(column, D)] = piece

    gather = Gather(place, full, (g_ring_s, g_ring_r, g_mate_s, g_mate_r, g_cross_s, g_cross_r))
    stage(MIX)
    ready()
    gather.start(MIX)

    me = rows(place.seq)
    three, seven = pl.ds(0, 3), pl.ds(0, count - 1)
    most = pl.ds(0, 3 * BLK)

    def group(n, sent, received):
        return Group(row_s.at[n], row_r.at[n], sent, received, place.mate)

    row_in = group(0, inputs.at[three], x.at[most])
    seg_in = group(1, seg_stage.at[three], segs.at[three])
    teach_in = group(2, teacher.at[three], low.at[most])
    out_go = group(3, out_rows.at[three], out_rows.at[three])
    back_go = group(4, back_rows.at[three], back_rows.at[three])
    seq_go = group(5, vec_seq.at[three], vec_seq.at[three])
    vec_in = Group(vec_s.at[0], vec_r.at[0], vec_all.at[seven], vec_all.at[seven], place.mate)
    vec_go = Group(vec_s.at[1], vec_r.at[1], vec_buf.at[seven], vec_buf.at[seven], place.mate)
    sq_go = Group(vec_s.at[2], vec_r.at[2], sq_buf.at[seven], sq_buf.at[seven], place.mate)
    for k in (2, 3, 1):
        peer = place.kin(k)
        row_in.start(inputs.at[peer[1]], x.at[me], peer)
    row_local = local(inputs.at[place.seq], x.at[me], row_l.at[0])
    seg_stage[...] = jnp.broadcast_to(segments[...][:, None, :], seg_stage.shape)
    vec_stage[...] = jnp.concatenate(
        [vec_ref[...].astype(BF).astype(F32), jnp.zeros((VROWS - vec_ref.shape[0], 128), F32)],
        axis=0,
    )
    for k in range(1, count):
        vec_in.start(vec_stage, vec_all.at[place.dp], place.dp_peer(k))
    for k in (2, 3, 1):
        peer = place.kin(k)
        seg_in.start(seg_stage.at[peer[1]], segs.at[place.seq], peer)
    for k in (2, 3, 1):
        peer = place.kin(k)
        teach_in.start(teacher.at[peer[1]], low.at[me], peer)
    segs[place.seq] = seg_stage[place.seq]
    vec_all[place.dp] = vec_stage[...]
    teach_local = local(teacher.at[place.seq], low.at[me], row_l.at[1])
    for w in (OUT, EXP, SHR):
        stage(w)

    def ring_steps(w, t):
        return [
            partial(gather.tick, w, lane, way, t)
            for lane in range(len(gather.lanes(w)))
            for way in range(2)
            if t <= place.hops[way]
        ]

    def relays(w, t):
        return [partial(gather.relay, w, way, t) for way in range(2) if 1 <= t <= place.hops[way]]

    far = place.hops[0]
    for t in range(1, far + 1):
        for step in ring_steps(MIX, t):
            step()
        if t == far - 2:
            gather.start(OUT)
        if t == far - 1:
            gather.start(EXP)
    for step in ring_steps(OUT, 1):
        step()

    vec_in.wait_recv()
    per = vec_ref.shape[0]
    flat = 0
    for name, size in VEC_PLACES:
        parts = []
        for r in range(flat, flat + size // 128):
            parts.append(vec_all[r // per, r % per : r % per + 1, :])
        vec[VEC_ROW[name] : VEC_ROW[name] + 1, 0:size] = jnp.concatenate(parts, axis=1)
        flat += size // 128

    def of(name):
        return vec[VEC_ROW[name] : VEC_ROW[name] + 1, 0 : VEC_SIZE[name]]

    def add_grad(name, term, start=0):
        gvec[VEC_ROW[name] : VEC_ROW[name] + 1, start : start + term.shape[1]] += term

    gvec[...] = jnp.zeros_like(gvec)
    row_local.wait()
    row_in.wait_recv()
    seg_in.wait_recv()

    for s in range(4):
        documents = jnp.concatenate([segs[s].astype(F32)] * 16, axis=0).T
        marked[s * BLK : (s + 1) * BLK, :] = document_lanes(documents)
    earlier = lax.broadcasted_iota(jnp.int32, (BLK, BLK), 0) <= lax.broadcasted_iota(
        jnp.int32, (BLK, BLK), 1
    )
    causal[...] = jnp.where(earlier, 0.0, NEGATIVE)

    def first_norm(i, _):
        hat, _ = normalised(x[rows(i), :].astype(F32))
        h1[rows(i), :] = (hat * of("g1") + of("b1")).astype(BF)
        return 0

    lax.fori_loop(0, blocks, first_norm, 0)
    gather.arrived(MIX)

    def lane(w, number, t):
        return [partial(gather.tick, w, number, way, t) for way in range(2) if t <= place.hops[way]]

    in_project = spread(
        [[], [], lane(EXP, 0, 1), [], [], lane(EXP, 1, 1), [], lane(OUT, 0, 2)],
        2,
    )
    in_forward = spread(
        [
            [],
            lane(EXP, 0, 2),
            lane(EXP, 1, 2) + lane(OUT, 0, 3),
            [],
            lane(EXP, 0, 3) + lane(OUT, 0, 4),
            lane(EXP, 1, 3) + [partial(gather.start, SHR)],
        ],
        1,
    )
    in_middle = spread([[], lane(EXP, 0, 4), [], lane(EXP, 1, 4)], 1)
    before_expand = relays(EXP, 1) + relays(EXP, 2) + lane(SHR, 0, 1) + relays(EXP, 3)
    before_expand += lane(SHR, 1, 1) + relays(EXP, 4)
    in_expand = spread(
        [
            lane(SHR, 2, 1), lane(SHR, 0, 2),
            [], lane(SHR, 1, 2),
            lane(SHR, 2, 2), lane(SHR, 0, 3),
            lane(SHR, 1, 3), [],
        ],
        2,
    )
    after_expand = lane(SHR, 2, 3) + lane(SHR, 0, 4) + lane(SHR, 1, 4) + lane(SHR, 2, 4)
    for t in range(1, far + 1):
        after_expand += relays(SHR, t)

    def project(i, _):
        in_project(i, 0)
        value = dot(h1[rows(i), :], whole(full[MIX]), NN)
        for part in range(2):
            c = slice(part * HALF, (part + 1) * HALF)
            q, k, v = (
                slice(part * 3 * HALF + n * HALF, part * 3 * HALF + (n + 1) * HALF) for n in range(3)
            )
            qkv[rows(i), q] = ((value[:, q] + of("bq")[:, c]) * scale).astype(BF)
            qkv[rows(i), k] = value[:, k].astype(BF)
            qkv[rows(i), v] = (value[:, v] + of("bv")[:, c]).astype(BF)
        in_project(i, 1)
        return 0

    lax.fori_loop(0, blocks, project, 0)
    def forward_pair(hp, _):
        attend_pair(
            hp,
            qkv,
            marked,
            causal,
            att,
            lse,
            dy,
            lambda i: in_forward(hp, 0) if i == 0 else None,
        )
        return 0

    lax.fori_loop(0, PAIRS, forward_pair, 0)
    def middle(i, _):
        in_middle(i, 0)
        value = x[rows(i), :].astype(F32) + dot(att[rows(i), :], whole(full[OUT]), NN) + of("bo")
        x1[rows(i), :] = value
        hat, _ = normalised(value)
        h2[rows(i), :] = (hat * of("g2") + of("b2")).astype(BF)
        return 0

    gather.arrived(OUT)
    lax.fori_loop(0, blocks, middle, 0)
    teach_local.wait()
    teach_in.wait_recv()

    def target(i, _):
        dy[rows(i), :] = softmax(low[rows(i), :].astype(F32))
        return 0

    for tick in before_expand[:6]:
        tick()
    lax.fori_loop(0, blocks, target, 0)
    for tick in before_expand[6:]:
        tick()
    gather.arrived(EXP)

    def expand(i, _):
        for n in range(FF // EXPAND_TILE):
            if n % 2 == 0:
                in_expand(i, n // 2)
            c = slice(n * EXPAND_TILE, (n + 1) * EXPAND_TILE)
            weight = full[EXP][:, :, :, c].reshape(D, EXPAND_TILE)
            u = dot(h2[rows(i), :], weight, NN) + vec[VEC_ROW["bf1"] : VEC_ROW["bf1"] + 1, c]
            a, s = gelu_both(u)
            act[rows(i), c] = a.astype(BF)
            slope[rows(i), c] = s.astype(BF)
        return 0

    lax.fori_loop(0, blocks, expand, 0)
    for tick in after_expand:
        tick()
    gather.arrived(SHR)

    def shrink(i, _):
        value = x1[rows(i), :] + dot(act[rows(i), :], whole(full[SHR]), NN) + of("bf2")
        sent[rows(i), :] = value.astype(BF)
        grad = D * (softmax(value) - dy[rows(i), :])
        dy[rows(i), :] = grad
        low[rows(i), :] = grad.astype(BF)
        add_grad("bf2", jnp.sum(grad, axis=0, keepdims=True))
        return 0

    lax.fori_loop(0, blocks, shrink, 0)
    for w in (MIX, OUT, EXP, SHR):
        gather.drain(w)

    def send_rows(rows_out, copies, k, first=0, size=BLK):
        peer = place.kin(k)
        source = sent.at[span(peer[1] * BLK + first, size, 128)]
        copies.start(source, rows_out.at[place.seq, pl.ds(first, size)], peer)

    out_local = local(sent.at[me], out_rows.at[place.seq], row_l.at[2])
    for k in (2, 3, 1):
        send_rows(out_rows, out_go, k)

    half, some = full[MIX].shape[2], count // 2

    def part_of(buffer, w, where):
        if w == EXP:
            return act.at[where]
        return slope.at[where, pl.ds(3 * D, D)]

    def third(group, n):
        return slope.at[span(n * 3 * half, 3 * half, 16), span(group * D, D, 128)]

    def mates(w, owner):
        if w == SHR:
            return shr_mate.at[owner]
        if w == MIX:
            return third(owner // (count // 2), owner % (count // 2))
        return part_of(act, w, span(owner * half, half, 16))

    def slots(w, t):
        if w == SHR:
            return shr_slot.at[t]
        if w == MIX:
            return third(2, t)
        return part_of(act, w, span((count + t) * half, half, 16))

    scatter = Scatter(
        place,
        (full3, full1, full2, shrink_grads),
        mates,
        slots,
        sums,
        (s_mate_s, s_mate_r, s_ring_s, s_ring_r, s_cross_s, s_cross_r, s_total_s, s_total_r),
    )

    def offer(which):
        for n, peer in enumerate((place.mate,) + place.sides):
            pl.semaphore_signal(
                free.at[3 * which + n], inc=1, device_id=peer, device_id_type=MESH
            )

    def accept(which, which_sides):
        for n in range(1, 3) if which_sides else range(1):
            pl.semaphore_wait(free.at[3 * which + n], 1)

    def shrink_grad(n, _):
        value = dot(act[:, span(n * D, D, 128)], low[...], TN).astype(BF)
        shrink_grads[pl.ds(2 * n, 2)] = value.reshape((2,) + shrink_grads.shape[1:])
        for owner in range(2):
            for sub in range(2):
                scatter.pair(SHR, sub, 2 * n + owner).start()
        return 0

    lax.fori_loop(0, FF // D, shrink_grad, 0)
    offer(0)
    for sub in range(2):
        scatter.start(SHR, sub)

    def hop(w, t, sub):
        return scatter.ticks(w, t, (sub,))

    def end(w, sub):
        return [partial(scatter.finish, w, sub)]

    in_middle_back = spread([hop(SHR, 1, 0), [], hop(SHR, 1, 1), []], 1)
    in_expand_grad = spread([hop(SHR, 2, 0), [], hop(SHR, 2, 1), []], 1)
    in_upstream = spread(
        [[partial(scatter.start, EXP, 0)] + hop(SHR, 3, 0), [], [partial(scatter.start, EXP, 1)], []],
        1,
    )
    in_backward = spread(
        [
            hop(SHR, 3, 1), [], [], [partial(scatter.start, OUT, 0)],
            hop(EXP, 1, 0), [], [], [],
            hop(EXP, 1, 1) + end(SHR, 0), [], [], hop(EXP, 2, 0) + hop(OUT, 1, 0) + end(SHR, 1),
            hop(EXP, 2, 1), [], [], [partial(scatter.start, MIX, 0)] + hop(OUT, 2, 0),
            hop(EXP, 3, 0), [], [], hop(EXP, 3, 1) + hop(OUT, 3, 0),
            hop(MIX, 1, 0), [], [], end(EXP, 0),
        ],
        4,
    )

    def expand_back(i, _):
        for n in range(FF // D):
            c = slice(n * D, (n + 1) * D)
            weight = full[SHR][2 * n : 2 * n + 2].reshape(D, D)
            da = dot(low[rows(i), :], weight, NT).astype(BF).astype(F32)
            du = (da * slope[rows(i), c].astype(F32)).astype(BF)
            slope[rows(i), c] = du
            gvec[VEC_ROW["bf1"] : VEC_ROW["bf1"] + 1, c] += jnp.sum(
                du.astype(F32), axis=0, keepdims=True
            )
        return 0

    lax.fori_loop(0, blocks, expand_back, 0)


    def middle_back(i, _):
        in_middle_back(i, 0)
        upstream = dot(slope[rows(i), :], whole(full[EXP]), NT)
        part, gain, shift = norm_grad(x1[rows(i), :], of("g2"), upstream)
        value = dy[rows(i), :] + part
        dy[rows(i), :] = value
        low[rows(i), :] = value.astype(BF)
        add_grad("g2", gain)
        add_grad("b2", shift)
        add_grad("bo", jnp.sum(value, axis=0, keepdims=True))
        return 0

    lax.fori_loop(0, blocks, middle_back, 0)
    accept(0, False)

    def expand_grad(n, _):
        in_expand_grad(n, 0)
        c = span(n * D, D, 128)
        for owners in range(2):
            value = dot(h2[:, owners * HALF : (owners + 1) * HALF], slope[:, c], TN).astype(BF)
            full2[owners * some : (owners + 1) * some, :, :, c] = value.reshape(
                (some,) + full2.shape[1:3] + (D,)
            )
        pl.when(n == FF // D // 2 - 1)(lambda: scatter.hand(EXP, 0))
        return 0

    lax.fori_loop(0, FF // D, expand_grad, 0)
    scatter.hand(EXP, 1)
    offer(1)
    accept(0, True)

    def upstream_rows(i, _):
        in_upstream(i, 0)
        h2[rows(i), :] = dot(low[rows(i), :], whole(full[OUT]), NT).astype(BF)
        return 0

    lax.fori_loop(0, blocks, upstream_rows, 0)
    for owners in range(2):
        value = dot(att[:, owners * HALF : (owners + 1) * HALF], low[...], TN).astype(BF)
        full1[owners * some : (owners + 1) * some] = value.reshape((some,) + full1.shape[1:])
    accept(1, False)
    scatter.hand(OUT, 0)
    accept(1, True)
    def backward_part(part, _):
        def backward_pair(hp, _):
            def tick(i):
                for n in range(2):
                    first = n * (PAIRS // 2)
                    pl.when(part == n)(
                        lambda first=first: in_backward(hp + first, i, first, first + PAIRS // 2)
                    )

            number = part * (PAIRS // 2) + hp
            attend_back_pair(
                number, qkv, marked, causal, att, h2, lse, x1, tick
            )
            return 0

        lax.fori_loop(0, PAIRS // 2, backward_pair, 0)
        c = span(part * 3 * HALF, 3 * HALF, 128)
        for owners in range(2):
            mine = slice(owners * HALF, (owners + 1) * HALF)
            value = dot(h1[:, mine], qkv[:, c], TN).astype(BF)
            for n in range(3):
                there = span(part * HALF, HALF, 128)
                full3[owners * some : (owners + 1) * some, :, n * half : (n + 1) * half, there] = (
                    value[:, n * HALF : (n + 1) * HALF].reshape(some, 2, half, HALF)
                )
        pl.when(part == 0)(lambda: scatter.hand(MIX, 0))
        pl.when(part == 1)(lambda: [scatter.hand(MIX, sub) for sub in range(1, 4)] and None)
        return 0

    lax.fori_loop(0, 2, backward_part, 0)
    for sub in range(1, 4):
        scatter.start(MIX, sub)
    for tick in hop(MIX, 2, 0) + end(EXP, 1) + end(OUT, 0):
        tick()
    out_local.wait()
    out_go.wait_send()
    in_input_back = spread([[], [], hop(MIX, 1, 1), hop(MIX, 1, 2) + hop(MIX, 1, 3)], 1)
    late = BLK // 2

    def input_back(j, _):
        in_input_back(j, 0)
        core = place.core + (1 - 2 * place.core) * (j % 2)
        i = 2 * (place.x + (1 - 2 * place.x) * (1 - j // 2)) + core
        d = qkv[rows(i), :]
        part, gain, shift = norm_grad(
            x[rows(i), :].astype(F32), of("g1"), dot(d, whole(full[MIX]), NT)
        )
        sent[rows(i), :] = (dy[rows(i), :] + part).astype(BF)
        add_grad("g1", gain)
        add_grad("b1", shift)
        for half_of in range(2):
            first = half_of * 3 * HALF
            for name, start in (("bq", first), ("bv", first + 2 * HALF)):
                term = d[:, start : start + HALF].astype(F32)
                add_grad(name, jnp.sum(term, axis=0, keepdims=True), half_of * HALF)
        pl.when(j == 0)(lambda: send_rows(back_rows, back_go, 2))
        pl.when(j == 1)(lambda: send_rows(back_rows, back_go, 3, 0, late))
        pl.when(j == 3)(lambda: send_rows(back_rows, back_go, 1))
        return 0

    lax.fori_loop(0, blocks, input_back, 0)
    back_local = local(sent.at[me], back_rows.at[place.seq], row_l.at[3])
    flat = 0
    vec_out[...] = jnp.zeros_like(vec_out)
    for name, size in VEC_PLACES:
        for n in range(size // 128):
            r = flat + n
            vec_out[r // per, r % per : r % per + 1, :] = gvec[
                VEC_ROW[name] : VEC_ROW[name] + 1, n * 128 : (n + 1) * 128
            ]
        flat += size // 128
    for k in range(1, count):
        peer = place.dp_peer(k)
        vec_go.start(vec_out.at[peer[0]], vec_buf.at[place.dp], peer)
    vec_buf[place.dp] = vec_out[place.dp]
    for tick in hop(MIX, 3, 0) + hop(MIX, 2, 1) + hop(MIX, 2, 2) + hop(MIX, 2, 3):
        tick()
    for w, sub in ((SHR, 0), (SHR, 1), (EXP, 0)):
        scatter.crossed(w, sub)
    for tick in hop(MIX, 3, 1) + hop(MIX, 3, 2) + hop(MIX, 3, 3) + end(MIX, 0):
        tick()
    vec_go.wait_recv()
    vec_mine[...] = jnp.sum(vec_buf[...], axis=0)
    vec_seq[place.seq] = vec_mine[...]
    for k in (2, 3, 1):
        seq_go.start(vec_mine, vec_seq.at[place.seq], place.kin(k))
    for sub in range(1, 4):
        scatter.finish(MIX, sub)
    send_rows(back_rows, back_go, 3, late, BLK - late)
    for w, sub in ((EXP, 1), (OUT, 0), (MIX, 0)):
        scatter.crossed(w, sub)

    def squares_of(w, part, total):
        c = slice(None) if part is None else slice(part * HALF, (part + 1) * HALF)
        for core in range(2):
            value = sums[w][core, :, c].astype(F32)
            term = jnp.sum(value * value, axis=0, keepdims=True)
            for n in range(term.shape[1] // 128):
                total = total + term[:, n * 128 : (n + 1) * 128]
        return total

    squares = jnp.zeros((1, 128), F32)
    for w in (SHR, EXP, OUT):
        for sub in range(SUBS[w]):
            scatter.arrived(w, sub)
        squares = squares_of(w, None, squares)
    scatter.arrived(MIX, 0)
    squares = squares_of(MIX, 0, squares)
    seq_go.wait_recv()
    vec_total = jnp.sum(vec_seq[...], axis=0)
    vec_sum[...] = vec_total
    squares = squares + jnp.sum(vec_total * vec_total, axis=0, keepdims=True)
    for sub in range(1, 4):
        scatter.crossed(MIX, sub)
    for sub in range(1, 4):
        scatter.arrived(MIX, sub)
    squares = squares_of(MIX, 1, squares)
    sq_mine[...] = jnp.broadcast_to(squares, sq_mine.shape)
    sq_buf[place.dp] = sq_mine[...]
    for k in range(1, count):
        sq_go.start(sq_mine, sq_buf.at[place.dp], place.dp_peer(k))
    for w in (MIX, OUT, EXP, SHR):
        scatter.drain(w)
    for copies in (row_in, seg_in, teach_in, vec_in, vec_go, seq_go, back_go, sq_go):
        copies.wait_send()
    back_local.wait()
    out_go.wait_recv()
    back_go.wait_recv()
    sq_go.wait_recv()
    total = jnp.sum(jnp.sum(sq_buf[...], axis=0), axis=1, keepdims=True)
    norm_ref[...] = jnp.broadcast_to(jnp.sqrt(total), norm_ref.shape)


def block_call(count, inputs, teacher, segments, masters, vectors):
    rows, local_len, features = inputs.shape
    length = rows * local_len
    halves = [(2, m.shape[0] // 2, m.shape[1]) for m in masters]
    any_spec = pl.BlockSpec(memory_space=pl.ANY)
    vmem = pl.BlockSpec(memory_space=pltpu.VMEM)
    row_shape = jax.ShapeDtypeStruct(inputs.shape, BF)
    folded = [(2, 3 * halves[MIX][1], D)] + halves[1:]
    out_shape = [jax.ShapeDtypeStruct(h, BF) for h in folded]
    out_shape += [
        jax.ShapeDtypeStruct((VROWS, 128), F32),
        jax.ShapeDtypeStruct((8, 128), F32),
        row_shape,
        row_shape,
    ]

    def low(*shape):
        return pltpu.VMEM(shape, BF)

    def wide(*shape):
        return pltpu.VMEM(shape, F32)

    def dma(*shape):
        return pltpu.SemaphoreType.DMA(shape)

    shrink_half = halves[SHR][1:]
    buffers = [low(count, *h) for h in halves]
    buffers += [
        low(length, D),
        low(length, D),
        low(length, 3 * D),
        low(length, D),
        wide(length, D),
        low(length, D),
        low(length, FF),
        low(length, FF),
        wide(length, D),
        low(length, D),
        low(length, D),
        low(count, *halves[SHR]),
        low(count, *shrink_half),
        low(count - 1, *shrink_half),
    ]
    buffers += [
        wide(16, length),
        pltpu.VMEM((rows, 8, local_len), jnp.int32),
        pltpu.VMEM((rows, 8, local_len), jnp.int32),
        low(length, 128),
        wide(BLK, BLK),
        wide(VROWS, 128),
        wide(count, VROWS, 128),
        wide(16, FF),
        wide(16, FF),
        wide(count, VROWS, 128),
        wide(count, VROWS, 128),
        wide(VROWS, 128),
        wide(4, VROWS, 128),
        wide(8, 128),
        wide(count, 8, 128),
    ]
    hops = count - 1
    sems = [dma(9), dma(4), dma(8, hops), dma(4), dma(4), dma(2), dma(2, hops)]
    sems += [dma(9), dma(9), dma(9), dma(9, hops)] + [dma(9)] * 4
    sems += [dma(6), dma(6), dma(4), dma(3), dma(3)]
    sems.append(pltpu.SemaphoreType.REGULAR((6,)))
    return pl.pallas_call(
        partial(block_kernel, count),
        out_shape=out_shape,
        in_specs=[any_spec] * 2 + [vmem] + [any_spec] * 4 + [vmem],
        out_specs=[vmem] * 6 + [any_spec] * 2,
        scratch_shapes=buffers + sems,
        compiler_params=pltpu.CompilerParams(
            collective_id=1, has_side_effects=True, vmem_limit_bytes=VMEM_BYTES
        ),
    )(inputs, teacher, segments, *masters, vectors.reshape(-1, 128))


def update_kernel(steps, norm_ref, *refs):
    sums, masters, firsts, seconds = refs[0:5], refs[5:10], refs[10:15], refs[15:20]
    out_from, back_from = refs[20:22]
    updated, first_out, second_out = refs[22:27], refs[27:32], refs[32:37]
    out_to, back_to, norm_out, held, sem = refs[37:42]
    step = pl.program_id(0)
    norm = norm_ref[0:1, 0:1]
    factor = clip_level() / jnp.maximum(norm, clip_level())
    takes = [
        pltpu.make_async_copy(rows, held.at[n], sem.at[n])
        for n, rows in enumerate((out_from, back_from))
    ]
    gives = [
        pltpu.make_async_copy(held.at[n], rows, sem.at[2 + n])
        for n, rows in enumerate((out_to, back_to))
    ]

    @pl.when(step == 0)
    def _():
        for copy in takes:
            copy.start()
        norm_out[...] = norm

    @pl.when(step == steps // 2)
    def _():
        for take, give in zip(takes, gives):
            take.wait()
            give.start()

    def apply(n, gradient):
        results = adamw(
            masters[n][...], firsts[n][...], seconds[n][...], gradient * factor, learn_rates()[n]
        )
        updated[n][...], first_out[n][...], second_out[n][...] = results

    for w in range(4):
        gradient = sums[w][...].astype(F32)
        if w == MIX:
            gradient = jnp.concatenate([gradient[n] for n in range(3)], axis=1)
        apply(w, gradient)

    @pl.when(step == 0)
    def _():
        apply(4, sums[4][0 : masters[4].shape[0], :])

    @pl.when(step == steps - 1)
    def _():
        for copy in gives:
            copy.wait()


def update_call(results, masters, firsts, seconds):
    half = results[OUT].shape[1]
    parts = half // 16
    steps = 2 * parts
    mixed = results[MIX].reshape(2, 3, half, D)

    def fixed(shape):
        return pl.BlockSpec(shape, lambda i: (0,) * len(shape))

    any_spec = pl.BlockSpec(memory_space=pl.ANY)
    sum_specs, state_specs, states = [], [], []
    for master in masters[:4]:
        rows, columns = master.shape[0] // steps, master.shape[1]
        sum_specs.append(pl.BlockSpec((None, rows, columns), lambda i: (i // parts, i % parts, 0)))
        state_specs.append(pl.BlockSpec((rows, columns), lambda i: (i, 0)))
    sum_specs[MIX] = pl.BlockSpec((None, 3, 16, D), lambda i: (i // parts, 0, i % parts, 0))
    packed = (masters[4].shape[0] // 128, 128)
    state_specs.append(fixed(packed))
    sum_specs.append(fixed(results[4].shape))
    for group in (masters, firsts, seconds):
        states += list(group[:4]) + [group[4].reshape(packed)]
    out_shape = [jax.ShapeDtypeStruct(state.shape, F32) for state in states]
    out_shape += [jax.ShapeDtypeStruct(results[6].shape, BF)] * 2
    out_shape.append(jax.ShapeDtypeStruct((1, 1), F32))
    return pl.pallas_call(
        partial(update_kernel, steps),
        grid=(steps,),
        out_shape=out_shape,
        in_specs=[fixed(results[5].shape)] + sum_specs + state_specs * 3 + [any_spec] * 2,
        out_specs=state_specs * 3 + [any_spec] * 2 + [fixed((1, 1))],
        scratch_shapes=[
            pltpu.VMEM((2,) + results[6].shape, BF),
            pltpu.SemaphoreType.DMA((4,)),
        ],
        compiler_params=pltpu.CompilerParams(vmem_limit_bytes=VMEM_BYTES),
    )(results[5], mixed, *results[1:5], *states, *results[6:8])


def row_body(
    inputs,
    segments,
    teacher,
    mixing_weight,
    output_weight,
    expand_weight,
    shrink_weight,
    vectors,
    mixing_first,
    output_first,
    expand_first,
    shrink_first,
    vectors_first,
    mixing_second,
    output_second,
    expand_second,
    shrink_second,
    vectors_second,
):
    masters = (mixing_weight, output_weight, expand_weight, shrink_weight, vectors)
    firsts = (mixing_first, output_first, expand_first, shrink_first, vectors_first)
    seconds = (mixing_second, output_second, expand_second, shrink_second, vectors_second)
    results = block_call(lax.axis_size("dp"), inputs, teacher, segments, masters[:4], vectors)
    fresh = update_call(results, masters, firsts, seconds)
    states = [
        state.reshape(vectors.shape) if n % 5 == 4 else state for n, state in enumerate(fresh[:15])
    ]
    return (fresh[15], fresh[16], fresh[17].reshape(()), *states)


def whole_rows(mesh):
    return mesh.shape["seq"] == 4 and mesh.shape["dp"] == 8


def solution(mesh):
    in_specs = (
        P("dp", "seq", None),
        P("dp", "seq"),
        P("dp", "seq", None),
        P("dp", None),
        P("dp", None),
        P("dp", None),
        P("dp", None),
        P("dp"),
        P("dp", None),
        P("dp", None),
        P("dp", None),
        P("dp", None),
        P("dp"),
        P("dp", None),
        P("dp", None),
        P("dp", None),
        P("dp", None),
        P("dp"),
    )
    out_specs = (
        P("dp", "seq", None),
        P("dp", "seq", None),
        P(),
        P("dp", None),
        P("dp", None),
        P("dp", None),
        P("dp", None),
        P("dp"),
        P("dp", None),
        P("dp", None),
        P("dp", None),
        P("dp", None),
        P("dp"),
        P("dp", None),
        P("dp", None),
        P("dp", None),
        P("dp", None),
        P("dp"),
    )
    chosen = row_body if whole_rows(mesh) else body
    return jax.shard_map(chosen, mesh=mesh, in_specs=in_specs, out_specs=out_specs, check_vma=False)
```

profile of v0, /device:TPU:0, one launch (start us, length us, event | category | flops | bytes accessed | tf_op | source)
XLA Modules:
  0.0 197.7 jit_solution(7683725015121469450)
XLA Ops:
  0.7 183.5 %shard_map.313 = (bf16[2,144,768]{2,1,0:T(8,128)(2,1)}, bf16[2,48,768]{2,1,0:T(8,128)(2,1)}, bf16[2,48,3072]{2,1,0:T(8,128)(2,1)}, bf16[2,192,768]{2,1,0:T(8,128...) custom-call(bf16[4,256,768]{2,1,0:T(8,128)(2,1)} %refs_0_.1, ...), custom_call_target="tpu_custom_call" | custom-call | tf_op jit(solution)/shard_map/pallas_call | solution.py:1464
  184.2 13.3 %shard_map.314 = (f32[96,2304]{1,0:T(8,128)}, f32[96,768]{1,0:T(8,128)}, f32[96,3072]{1,0:T(8,128)}, f32[384,768]{1,0:T(8,128)}, f32[9,128]{1,0:T(8,128)}, /*ind...) custom-call(f32[8,128]{1,0:T(8,128)} %get-tuple-element.44.norm_ref,, ...), custom_call_target="tpu_custom_call" | custom-call | tf_op jit(solution)/shard_map/pallas_call | solution.py:1551
where the time goes:
time: 198 us
  Pallas kernels  197 us (99%)
    pallas_call x1, Pallas kernels, block_call(): pl.pallas_call(partial(block_kernel, count), out_shape=out_shape, in_spec...  184 us
    pallas_call x1, Pallas kernels, update_call(): pl.pallas_call(partial(update_kernel, steps), grid=(steps,), out_shape=ou...  13.3 us

commit v1 on v0

--- a/solution.py
+++ b/solution.py
@@ -436,7 +436,7 @@
         self.ring_s, self.ring_r, self.mate_s, self.mate_r, self.cross_s, self.cross_r = sems
 
     def lanes(self, w):
-        return ((0, 1), (0,), (self.place.x, 2), (self.place.x, 2, 3))[w]
+        return ((0, 1, 2), (0,), (self.place.x, 2, 3), (self.place.x, 2, 3))[w]
 
     def part(self, ref, w, sub):
         rows, columns = ref.shape[-2:]
@@ -446,7 +446,7 @@
             if isinstance(sub, int) and sub >= 2:
                 return ref.at[lead + (pl.ds((2 * sub - 2) * unit, 2 * unit),)]
             return ref.at[lead + (span(sub * unit, unit, 16),)]
-        unit = columns // (2, 1, 3)[w]
+        unit = columns // (3, 1, 4)[w]
         return ref.at[lead + (slice(None), span(sub * unit, unit, 128))]
 
     def cut(self, w, owner, core, sub):
@@ -460,7 +460,7 @@
         return describe(block, block, send, recv, device)
 
     def ring(self, w, lane, way, t):
-        index = ((0, 2, 3, 5)[w] + lane, t + way * self.place.hops[0])
+        index = ((0, 3, 4, 7)[w] + lane, t + way * self.place.hops[0])
         block = self.block(w, self.lanes(w)[lane], way, t)
         return self.copy(block, self.ring_s.at[w], self.ring_r.at[index], self.place.sides[way])
 
@@ -853,16 +853,17 @@
 
 def block_kernel(count, *refs):
     inputs, teacher, segments, masters, vec_ref = refs[0], refs[1], refs[2], refs[3:7], refs[7]
-    sums, vec_sum, norm_ref, out_rows, back_rows = refs[8:12], refs[12], refs[13], refs[14], refs[15]
+    sums_out, vec_sum, norm_ref, out_rows, back_rows = refs[8:12], *refs[12:16]
     (
         full0, full1, full2, full3, x, h1, qkv, att, x1, h2, act, slope, dy, low, sent, shrink_grads,
         shr_mate, shr_slot, lse, segs, seg_stage, marked, causal,
-        vec_stage, vec_all, vec, gvec, vec_out, vec_buf, vec_mine, vec_seq, sq_mine, sq_buf,
+        sums0, sums1, sums2, sums3, vec_stage, vec_all, vec, gvec, vec_out, vec_buf, vec_mine, vec_seq, sq_mine, sq_buf,
         load_sem, g_ring_s, g_ring_r, g_mate_s, g_mate_r, g_cross_s, g_cross_r,
         s_mate_s, s_mate_r, s_ring_s, s_ring_r, s_cross_s, s_cross_r, s_total_s, s_total_r,
         row_s, row_r, row_l, vec_s, vec_r, free,
     ) = refs[16:]
     full = (full0, full1, full2, full3)
+    sums = (sums0, sums1, sums2, sums3)
     place = Place(count)
     ready = place.greet()
     length = x.shape[0]
@@ -931,9 +932,15 @@
     for k in (2, 3, 1):
         peer = place.kin(k)
         seg_in.start(seg_stage.at[peer[1]], segs.at[place.seq], peer)
-    for k in (2, 3, 1):
+
+    def send_teacher(k, part=0, parts=1):
+        size = BLK // parts
+        there = low.at[span(place.seq * BLK + part * size, size, 16)]
         peer = place.kin(k)
-        teach_in.start(teacher.at[peer[1]], low.at[me], peer)
+        teach_in.start(teacher.at[peer[1], pl.ds(part * size, size)], there, peer)
+
+    for k in (2, 1):
+        send_teacher(k)
     segs[place.seq] = seg_stage[place.seq]
     vec_all[place.dp] = vec_stage[...]
     teach_local = local(teacher.at[place.seq], low.at[me], row_l.at[1])
@@ -1002,34 +1009,37 @@
     def lane(w, number, t):
         return [partial(gather.tick, w, number, way, t) for way in range(2) if t <= place.hops[way]]
 
+    def piece(n):
+        return [partial(send_teacher, 3, n, 4)]
+
     in_project = spread(
-        [[], [], lane(EXP, 0, 1), [], [], lane(EXP, 1, 1), [], lane(OUT, 0, 2)],
+        [[], [], lane(EXP, 0, 1), lane(EXP, 1, 1), piece(0), lane(EXP, 2, 1), [], lane(OUT, 0, 2)],
         2,
     )
     in_forward = spread(
         [
             [],
-            lane(EXP, 0, 2),
-            lane(EXP, 1, 2) + lane(OUT, 0, 3),
-            [],
-            lane(EXP, 0, 3) + lane(OUT, 0, 4),
-            lane(EXP, 1, 3) + [partial(gather.start, SHR)],
+            lane(EXP, 0, 2) + piece(1),
+            lane(EXP, 1, 2) + lane(EXP, 2, 2),
+            lane(OUT, 0, 3),
+            lane(EXP, 0, 3) + lane(OUT, 0, 4) + piece(2),
+            lane(EXP, 1, 3) + lane(EXP, 2, 3) + [partial(gather.start, SHR)],
         ],
         1,
     )
-    in_middle = spread([[], lane(EXP, 0, 4), [], lane(EXP, 1, 4)], 1)
+    in_middle = spread([[], lane(EXP, 0, 4) + piece(3), lane(EXP, 1, 4), lane(EXP, 2, 4)], 1)
     before_expand = relays(EXP, 1) + relays(EXP, 2) + lane(SHR, 0, 1) + relays(EXP, 3)
     before_expand += lane(SHR, 1, 1) + relays(EXP, 4)
     in_expand = spread(
         [
             lane(SHR, 2, 1), lane(SHR, 0, 2),
             [], lane(SHR, 1, 2),
-            lane(SHR, 2, 2), lane(SHR, 0, 3),
-            lane(SHR, 1, 3), [],
+            lane(SHR, 2, 2) + lane(SHR, 0, 3), [],
+            lane(SHR, 1, 3), lane(SHR, 0, 4) + lane(SHR, 2, 3),
         ],
         2,
     )
-    after_expand = lane(SHR, 2, 3) + lane(SHR, 0, 4) + lane(SHR, 1, 4) + lane(SHR, 2, 4)
+    after_expand = lane(SHR, 1, 4) + lane(SHR, 2, 4)
     for t in range(1, far + 1):
         after_expand += relays(SHR, t)
 
@@ -1072,18 +1082,16 @@
 
     gather.arrived(OUT)
     lax.fori_loop(0, blocks, middle, 0)
-    teach_local.wait()
-    teach_in.wait_recv()
 
     def target(i, _):
         dy[rows(i), :] = softmax(low[rows(i), :].astype(F32))
         return 0
 
-    for tick in before_expand[:6]:
+    for tick in before_expand:
         tick()
+    teach_local.wait()
+    teach_in.wait_recv()
     lax.fori_loop(0, blocks, target, 0)
-    for tick in before_expand[6:]:
-        tick()
     gather.arrived(EXP)
 
     def expand(i, _):
@@ -1178,8 +1186,6 @@
 
     lax.fori_loop(0, FF // D, shrink_grad, 0)
     offer(0)
-    for sub in range(2):
-        scatter.start(SHR, sub)
 
     def hop(w, t, sub):
         return scatter.ticks(w, t, (sub,))
@@ -1190,22 +1196,25 @@
     in_middle_back = spread([hop(SHR, 1, 0), [], hop(SHR, 1, 1), []], 1)
     in_expand_grad = spread([hop(SHR, 2, 0), [], hop(SHR, 2, 1), []], 1)
     in_upstream = spread(
-        [[partial(scatter.start, EXP, 0)] + hop(SHR, 3, 0), [], [partial(scatter.start, EXP, 1)], []],
+        [[partial(scatter.start, EXP, 0)] + hop(SHR, 3, 0), [], [], []],
         1,
     )
     in_backward = spread(
         [
             hop(SHR, 3, 1), [], [], [partial(scatter.start, OUT, 0)],
-            hop(EXP, 1, 0), [], [], [],
-            hop(EXP, 1, 1) + end(SHR, 0), [], [], hop(EXP, 2, 0) + hop(OUT, 1, 0) + end(SHR, 1),
-            hop(EXP, 2, 1), [], [], [partial(scatter.start, MIX, 0)] + hop(OUT, 2, 0),
-            hop(EXP, 3, 0), [], [], hop(EXP, 3, 1) + hop(OUT, 3, 0),
-            hop(MIX, 1, 0), [], [], end(EXP, 0),
+            hop(EXP, 1, 0) + end(SHR, 0), [], [], [],
+            hop(EXP, 1, 1) + hop(OUT, 1, 0), [], [], hop(EXP, 2, 0) + end(SHR, 1),
+            hop(OUT, 2, 0) + hop(EXP, 2, 1), [], [], hop(EXP, 3, 0) + [partial(scatter.start, MIX, 0)],
+            [], [], [], hop(OUT, 3, 0) + hop(EXP, 3, 1),
+            end(EXP, 0), [], [], hop(MIX, 1, 0) + end(OUT, 0) + end(EXP, 1),
         ],
         4,
     )
 
+    in_expand_back = spread([[], [partial(scatter.start, SHR, sub) for sub in range(2)], [], []], 1)
+
     def expand_back(i, _):
+        in_expand_back(i, 0)
         for n in range(FF // D):
             c = slice(n * D, (n + 1) * D)
             weight = full[SHR][2 * n : 2 * n + 2].reshape(D, D)
@@ -1258,6 +1267,8 @@
 
     lax.fori_loop(0, blocks, upstream_rows, 0)
     for owners in range(2):
+        if owners:
+            scatter.start(EXP, 1)
         value = dot(att[:, owners * HALF : (owners + 1) * HALF], low[...], TN).astype(BF)
         full1[owners * some : (owners + 1) * some] = value.reshape((some,) + full1.shape[1:])
     accept(1, False)
@@ -1288,18 +1299,30 @@
                 full3[owners * some : (owners + 1) * some, :, n * half : (n + 1) * half, there] = (
                     value[:, n * HALF : (n + 1) * HALF].reshape(some, 2, half, HALF)
                 )
-        pl.when(part == 0)(lambda: scatter.hand(MIX, 0))
-        pl.when(part == 1)(lambda: [scatter.hand(MIX, sub) for sub in range(1, 4)] and None)
+            for number in range(2):
+
+                def hand(number=number, owners=owners):
+                    for sub in ((0,), (1, 2, 3))[number]:
+                        for owner in range(owners * some, (owners + 1) * some):
+                            scatter.pair(MIX, sub, owner).start()
+
+                pl.when(part == number)(hand)
         return 0
 
     lax.fori_loop(0, 2, backward_part, 0)
-    for sub in range(1, 4):
-        scatter.start(MIX, sub)
-    for tick in hop(MIX, 2, 0) + end(EXP, 1) + end(OUT, 0):
+    for tick in hop(MIX, 2, 0):
         tick()
     out_local.wait()
     out_go.wait_send()
-    in_input_back = spread([[], [], hop(MIX, 1, 1), hop(MIX, 1, 2) + hop(MIX, 1, 3)], 1)
+    in_input_back = spread(
+        [
+            [],
+            [partial(scatter.start, MIX, sub) for sub in range(1, 4)],
+            hop(MIX, 3, 0),
+            hop(MIX, 1, 1),
+        ],
+        1,
+    )
     late = BLK // 2
 
     def input_back(j, _):
@@ -1319,7 +1342,7 @@
                 term = d[:, start : start + HALF].astype(F32)
                 add_grad(name, jnp.sum(term, axis=0, keepdims=True), half_of * HALF)
         pl.when(j == 0)(lambda: send_rows(back_rows, back_go, 2))
-        pl.when(j == 1)(lambda: send_rows(back_rows, back_go, 3, 0, late))
+        pl.when(j == 1)(lambda: send_rows(back_rows, back_go, 3, 0, late) if late else None)
         pl.when(j == 3)(lambda: send_rows(back_rows, back_go, 1))
         return 0
 
@@ -1338,11 +1361,11 @@
         peer = place.dp_peer(k)
         vec_go.start(vec_out.at[peer[0]], vec_buf.at[place.dp], peer)
     vec_buf[place.dp] = vec_out[place.dp]
-    for tick in hop(MIX, 3, 0) + hop(MIX, 2, 1) + hop(MIX, 2, 2) + hop(MIX, 2, 3):
+    for tick in hop(MIX, 1, 2) + hop(MIX, 1, 3) + end(MIX, 0) + hop(MIX, 2, 1) + hop(MIX, 2, 2) + hop(MIX, 2, 3):
         tick()
     for w, sub in ((SHR, 0), (SHR, 1), (EXP, 0)):
         scatter.crossed(w, sub)
-    for tick in hop(MIX, 3, 1) + hop(MIX, 3, 2) + hop(MIX, 3, 3) + end(MIX, 0):
+    for tick in hop(MIX, 3, 1) + hop(MIX, 3, 2) + hop(MIX, 3, 3):
         tick()
     vec_go.wait_recv()
     vec_mine[...] = jnp.sum(vec_buf[...], axis=0)
@@ -1384,11 +1407,13 @@
     sq_buf[place.dp] = sq_mine[...]
     for k in range(1, count):
         sq_go.start(sq_mine, sq_buf.at[place.dp], place.dp_peer(k))
+    saved = [local(sums[w], sums_out[w], load_sem.at[w]) for w in range(4)]
     for w in (MIX, OUT, EXP, SHR):
         scatter.drain(w)
     for copies in (row_in, seg_in, teach_in, vec_in, vec_go, seq_go, back_go, sq_go):
         copies.wait_send()
-    back_local.wait()
+    for copy in saved + [back_local]:
+        copy.wait()
     out_go.wait_recv()
     back_go.wait_recv()
     sq_go.wait_recv()
@@ -1445,6 +1470,7 @@
         pltpu.VMEM((rows, 8, local_len), jnp.int32),
         low(length, 128),
         wide(BLK, BLK),
+        *(low(*shape) for shape in folded),
         wide(VROWS, 128),
         wide(count, VROWS, 128),
         wide(16, FF),
@@ -1457,7 +1483,7 @@
         wide(count, 8, 128),
     ]
     hops = count - 1
-    sems = [dma(9), dma(4), dma(8, hops), dma(4), dma(4), dma(2), dma(2, hops)]
+    sems = [dma(9), dma(4), dma(10, hops), dma(4), dma(4), dma(2), dma(2, hops)]
     sems += [dma(9), dma(9), dma(9), dma(9, hops)] + [dma(9)] * 4
     sems += [dma(6), dma(6), dma(4), dma(3), dma(3)]
     sems.append(pltpu.SemaphoreType.REGULAR((6,)))
@@ -1465,7 +1491,7 @@
         partial(block_kernel, count),
         out_shape=out_shape,
         in_specs=[any_spec] * 2 + [vmem] + [any_spec] * 4 + [vmem],
-        out_specs=[vmem] * 6 + [any_spec] * 2,
+        out_specs=[any_spec] * 4 + [vmem] * 2 + [any_spec] * 2,
         scratch_shapes=buffers + sems,
         compiler_params=pltpu.CompilerParams(
             collective_id=1, has_side_effects=True, vmem_limit_bytes=VMEM_BYTES
@@ -1503,10 +1529,15 @@
             give.start()
 
     def apply(n, gradient):
-        results = adamw(
-            masters[n][...], firsts[n][...], seconds[n][...], gradient * factor, learn_rates()[n]
-        )
-        updated[n][...], first_out[n][...], second_out[n][...] = results
+        rate = learn_rates()[n]
+        clipped = gradient * factor
+        first = BETA_ONE * firsts[n][...] + (1.0 - BETA_ONE) * clipped
+        second = BETA_TWO * seconds[n][...] + (1.0 - BETA_TWO) * (clipped * clipped)
+        scale = jnp.sqrt(second * (1.0 / (1.0 - BETA_TWO**STEP))) + ADAM_EPS
+        change = first * (rate / (1.0 - BETA_ONE**STEP)) / scale
+        updated[n][...] = masters[n][...] * (1.0 - rate * WEIGHT_DECAY) - change
+        first_out[n][...] = first
+        second_out[n][...] = second
 
     for w in range(4):
         gradient = sums[w][...].astype(F32)
@@ -1526,7 +1557,7 @@
 
 def update_call(results, masters, firsts, seconds):
     half = results[OUT].shape[1]
-    parts = half // 16
+    parts = 1
     steps = 2 * parts
     mixed = results[MIX].reshape(2, 3, half, D)
 
@@ -1539,7 +1570,9 @@
         rows, columns = master.shape[0] // steps, master.shape[1]
         sum_specs.append(pl.BlockSpec((None, rows, columns), lambda i: (i // parts, i % parts, 0)))
         state_specs.append(pl.BlockSpec((rows, columns), lambda i: (i, 0)))
-    sum_specs[MIX] = pl.BlockSpec((None, 3, 16, D), lambda i: (i // parts, 0, i % parts, 0))
+    sum_specs[MIX] = pl.BlockSpec(
+        (None, 3, half // parts, D), lambda i: (i // parts, 0, i % parts, 0)
+    )
     packed = (masters[4].shape[0] // 128, 128)
     state_specs.append(fixed(packed))
     sum_specs.append(fixed(results[4].shape))

time: 198 us -> 190 us (0.960)
  Pallas kernels: 197 us -> 189 us
    pallas_call x1, Pallas kernels: 184 us -> 178 us  [block_call(): pl.pallas_call(partial(block_kernel, count), out_shape=out_shape, in_spec...]
where the time goes in v1:
time: 190 us
  Pallas kernels  189 us (99%)
    pallas_call x1, Pallas kernels, block_call(): pl.pallas_call(partial(block_kernel, count), out_shape=out_shape, in_spec...  178 us
    pallas_call x1, Pallas kernels, update_call(): pl.pallas_call(partial(update_kernel, steps), grid=(steps,), out_shape=ou...  11.4 us

profile of v1, /device:TPU:0, one launch (start us, length us, event | category | flops | bytes accessed | tf_op | source)
XLA Modules:
  0.0 189.8 jit_solution(8943144754991295651)
XLA Ops:
  0.7 177.6 %shard_map.313 = (bf16[2,144,768]{2,1,0:T(8,128)(2,1)}, bf16[2,48,768]{2,1,0:T(8,128)(2,1)}, bf16[2,48,3072]{2,1,0:T(8,128)(2,1)}, bf16[2,192,768]{2,1,0:T(8,128...) custom-call(bf16[4,256,768]{2,1,0:T(8,128)(2,1)} %refs_0_.1, ...), custom_call_target="tpu_custom_call" | custom-call | tf_op jit(solution)/shard_map/pallas_call | solution.py:1490
  178.2 11.4 %shard_map.314 = (f32[96,2304]{1,0:T(8,128)}, f32[96,768]{1,0:T(8,128)}, f32[96,3072]{1,0:T(8,128)}, f32[384,768]{1,0:T(8,128)}, f32[9,128]{1,0:T(8,128)}, /*ind...) custom-call(f32[8,128]{1,0:T(8,128)} %get-tuple-element.44.norm_ref,, ...), custom_call_target="tpu_custom_call" | custom-call | tf_op jit(solution)/shard_map/pallas_call | solution.py:1584

commit v2 on v1

--- a/solution.py
+++ b/solution.py
@@ -442,9 +442,7 @@
         rows, columns = ref.shape[-2:]
         lead = (slice(None),) * (len(ref.shape) - 2)
         if w == SHR:
-            unit = rows // 6
-            if isinstance(sub, int) and sub >= 2:
-                return ref.at[lead + (pl.ds((2 * sub - 2) * unit, 2 * unit),)]
+            unit = rows // 4
             return ref.at[lead + (span(sub * unit, unit, 16),)]
         unit = columns // (3, 1, 4)[w]
         return ref.at[lead + (slice(None), span(sub * unit, unit, 128))]
@@ -1033,9 +1031,9 @@
     in_expand = spread(
         [
             lane(SHR, 2, 1), lane(SHR, 0, 2),
-            [], lane(SHR, 1, 2),
-            lane(SHR, 2, 2) + lane(SHR, 0, 3), [],
-            lane(SHR, 1, 3), lane(SHR, 0, 4) + lane(SHR, 2, 3),
+            lane(SHR, 1, 2), lane(SHR, 2, 2),
+            lane(SHR, 0, 3), lane(SHR, 1, 3),
+            lane(SHR, 2, 3), lane(SHR, 0, 4),
         ],
         2,
     )
@@ -1201,11 +1199,11 @@
     )
     in_backward = spread(
         [
-            hop(SHR, 3, 1), [], [], [partial(scatter.start, OUT, 0)],
-            hop(EXP, 1, 0) + end(SHR, 0), [], [], [],
-            hop(EXP, 1, 1) + hop(OUT, 1, 0), [], [], hop(EXP, 2, 0) + end(SHR, 1),
-            hop(OUT, 2, 0) + hop(EXP, 2, 1), [], [], hop(EXP, 3, 0) + [partial(scatter.start, MIX, 0)],
-            [], [], [], hop(OUT, 3, 0) + hop(EXP, 3, 1),
+            hop(SHR, 3, 1), [], [], [],
+            [partial(scatter.start, OUT, 0)] + hop(EXP, 1, 0) + end(SHR, 0), [], [], [],
+            hop(EXP, 1, 1), [], [], hop(EXP, 2, 0) + hop(OUT, 1, 0) + end(SHR, 1),
+            hop(EXP, 2, 1), [], [], hop(OUT, 2, 0) + hop(EXP, 3, 0) + [partial(scatter.start, MIX, 0)],
+            [], [], [], hop(EXP, 3, 1) + hop(OUT, 3, 0),
             end(EXP, 0), [], [], hop(MIX, 1, 0) + end(OUT, 0) + end(EXP, 1),
         ],
         4,

time: 190 us -> 188 us (0.989)
  Pallas kernels: 189 us -> 187 us
    pallas_call x1, Pallas kernels: 178 us -> 175 us  [block_call(): pl.pallas_call(partial(block_kernel, count), out_shape=out_shape, in_spec...]
where the time goes in v2:
time: 188 us
  Pallas kernels  187 us (99%)
    pallas_call x1, Pallas kernels, block_call(): pl.pallas_call(partial(block_kernel, count), out_shape=out_shape, in_spec...  175 us
    pallas_call x1, Pallas kernels, update_call(): pl.pallas_call(partial(update_kernel, steps), grid=(steps,), out_shape=ou...  11.4 us

profile of v2, /device:TPU:0, one launch (start us, length us, event | category | flops | bytes accessed | tf_op | source)
XLA Modules:
  0.0 187.7 jit_solution(9419270700406265421)
XLA Ops:
  0.7 175.5 %shard_map.313 = (bf16[2,144,768]{2,1,0:T(8,128)(2,1)}, bf16[2,48,768]{2,1,0:T(8,128)(2,1)}, bf16[2,48,3072]{2,1,0:T(8,128)(2,1)}, bf16[2,192,768]{2,1,0:T(8,128...) custom-call(bf16[4,256,768]{2,1,0:T(8,128)(2,1)} %refs_0_.1, ...), custom_call_target="tpu_custom_call" | custom-call | tf_op jit(solution)/shard_map/pallas_call | solution.py:1488
  176.1 11.4 %shard_map.314 = (f32[96,2304]{1,0:T(8,128)}, f32[96,768]{1,0:T(8,128)}, f32[96,3072]{1,0:T(8,128)}, f32[384,768]{1,0:T(8,128)}, f32[9,128]{1,0:T(8,128)}, /*ind...) custom-call(f32[8,128]{1,0:T(8,128)} %get-tuple-element.44.norm_ref,, ...), custom_call_target="tpu_custom_call" | custom-call | tf_op jit(solution)/shard_map/pallas_call | solution.py:1582

commit v3 on v2

--- a/solution.py
+++ b/solution.py
@@ -1021,11 +1021,11 @@
             lane(EXP, 1, 2) + lane(EXP, 2, 2),
             lane(OUT, 0, 3),
             lane(EXP, 0, 3) + lane(OUT, 0, 4) + piece(2),
-            lane(EXP, 1, 3) + lane(EXP, 2, 3) + [partial(gather.start, SHR)],
+            lane(EXP, 1, 3) + lane(EXP, 2, 3) + piece(3) + [partial(gather.start, SHR)],
         ],
         1,
     )
-    in_middle = spread([[], lane(EXP, 0, 4) + piece(3), lane(EXP, 1, 4), lane(EXP, 2, 4)], 1)
+    in_middle = spread([[], lane(EXP, 0, 4), lane(EXP, 1, 4), lane(EXP, 2, 4)], 1)
     before_expand = relays(EXP, 1) + relays(EXP, 2) + lane(SHR, 0, 1) + relays(EXP, 3)
     before_expand += lane(SHR, 1, 1) + relays(EXP, 4)
     in_expand = spread(
@@ -1085,11 +1085,12 @@
         dy[rows(i), :] = softmax(low[rows(i), :].astype(F32))
         return 0
 
-    for tick in before_expand:
+    for tick in before_expand[:-1]:
         tick()
     teach_local.wait()
     teach_in.wait_recv()
     lax.fori_loop(0, blocks, target, 0)
+    before_expand[-1]()
     gather.arrived(EXP)
 
     def expand(i, _):

time: 188 us -> 188 us (level)
  no operation moved by 1% of the time
where the time goes in v3:
time: 188 us
  Pallas kernels  187 us (99%)
    pallas_call x1, Pallas kernels, block_call(): pl.pallas_call(partial(block_kernel, count), out_shape=out_shape, in_spec...  176 us
    pallas_call x1, Pallas kernels, update_call(): pl.pallas_call(partial(update_kernel, steps), grid=(steps,), out_shape=ou...  11.4 us

profile of v3, /device:TPU:0, one launch (start us, length us, event | category | flops | bytes accessed | tf_op | source)
XLA Modules:
  0.0 187.8 jit_solution(654219899793989868)
XLA Ops:
  0.7 175.6 %shard_map.313 = (bf16[2,144,768]{2,1,0:T(8,128)(2,1)}, bf16[2,48,768]{2,1,0:T(8,128)(2,1)}, bf16[2,48,3072]{2,1,0:T(8,128)(2,1)}, bf16[2,192,768]{2,1,0:T(8,128...) custom-call(bf16[4,256,768]{2,1,0:T(8,128)(2,1)} %refs_0_.1, ...), custom_call_target="tpu_custom_call" | custom-call | tf_op jit(solution)/shard_map/pallas_call | solution.py:1489
  176.2 11.4 %shard_map.314 = (f32[96,2304]{1,0:T(8,128)}, f32[96,768]{1,0:T(8,128)}, f32[96,3072]{1,0:T(8,128)}, f32[384,768]{1,0:T(8,128)}, f32[9,128]{1,0:T(8,128)}, /*ind...) custom-call(f32[8,128]{1,0:T(8,128)} %get-tuple-element.44.norm_ref,, ...), custom_call_target="tpu_custom_call" | custom-call | tf_op jit(solution)/shard_map/pallas_call | solution.py:1583
